TPU v7x, 256 devices: a whole 4x4x8 slice. The times are simulated.
256 devices in a mesh: scene: 64 (over x, z, core), strip: 4 (over y).
Axes of the slice: x: 4, y: 4, z: 8, core: 2. Of those that a mesh axis runs over, the one named last changes fastest.
Arguments:
- scene_tiles: bfloat16 [384, 10, 2, 4096], P('scene', None, None, 'strip')
- scene_slot: int32 [320], replicated, may hold values from 0 to 383, as said below
- pair_ref: int32 [4096], P('scene'), may hold values from 0 to 319, as said below
- pair_sec: int32 [4096], P('scene'), may hold values from 0 to 319, as said below
- pair_count: int32 [64], P('scene'), may hold values from 1 to 64, 2560 in all
Outputs:
- coherence: float32 [4096, 2, 2, 1024], P('scene', None, None, 'strip')
Inputs may be any that keep to these rules, and one draw needn't show every extreme that they name: `scene_slot`: distinct slots; each block of 6 aligned slots holds at least one scene. `pair_ref`: within the 64 pair slots of one index of scene, the reference and secondary scenes held in the slots of any one index of scene are used at most 2 times together, and exactly so for some; a pair's two scenes differ. `pair_sec`: see pair_ref.
All inputs are finite; a program needn't handle non-finite values. No bound on the sum of `pair_count` on one device may be relied on, other than what follows from the above.
Results may differ from a plain program's by a relative error of at most 0.0003.
Values may be sent and summed in bfloat16 or wider, within the bound.
A program may use at most 64 MiB of HBM per device.

v0:
```python
import jax
import jax.numpy as jnp
from jax import lax
from jax.sharding import PartitionSpec as P


def extended(block, sides, width):
    for axis, dim in sides:
        count = lax.axis_size(axis)
        forward = [(i, i + 1) for i in range(count - 1)]
        backward = [(target, source) for source, target in forward]
        low = lax.ppermute(
            lax.slice_in_dim(block, block.shape[dim] - width, None, axis=dim), axis, forward
        )
        high = lax.ppermute(lax.slice_in_dim(block, 0, width, axis=dim), axis, backward)
        block = jnp.concatenate([low, block, high], axis=dim)
    return block


def shards(scene_tiles, scene_slot, pair_ref, pair_sec, pair_count):
    pcap = pair_ref.shape[0]
    own_list = jnp.concatenate([pair_ref, pair_sec])
    own_slot = scene_slot[own_list]
    piece = lax.all_gather(scene_tiles, "scene", axis=0, tiled=True)
    rows = piece.shape[0]
    hit = jnp.where(
        own_slot[:, None] == jnp.arange(rows, dtype=jnp.int32)[None, :], 1.0, 0.0
    ).astype(jnp.bfloat16)
    found = jnp.einsum("js,sazr->jazr", hit, piece, preferred_element_type=jnp.float32)
    fetched = found.astype(jnp.bfloat16)
    lines_az = scene_tiles.shape[1]
    range_dev = scene_tiles.shape[3]
    a0 = fetched[:pcap, :, 0].astype(jnp.float32)
    a1 = fetched[:pcap, :, 1].astype(jnp.float32)
    b0 = fetched[pcap:, :, 0].astype(jnp.float32)
    b1 = fetched[pcap:, :, 1].astype(jnp.float32)
    planes = jnp.stack(
        [a0 * b0 + a1 * b1, a1 * b0 - a0 * b1, a0 * a0 + a1 * a1, b0 * b0 + b1 * b1], axis=1
    )
    summed = planes.reshape(pcap, 4, lines_az // 5, 5, range_dev).sum(axis=3)
    widened = extended(summed, (("strip", 3),), 10)
    blocks = widened.reshape(pcap, 4, lines_az // 5, (range_dev + 20) // 4, 4).sum(axis=4)
    count = range_dev // 4
    looks = (
        blocks[..., 0:count]
        + blocks[..., 1 : count + 1]
        + blocks[..., 2 : count + 2]
        + blocks[..., 3 : count + 3]
        + blocks[..., 4 : count + 4]
    )
    denom = jnp.sqrt(looks[:, 2] * looks[:, 3] + 1e-06)
    result = jnp.stack([looks[:, 0] / denom, looks[:, 1] / denom], axis=2)
    live = jnp.arange(pcap) < pair_count[0]
    return jnp.where(live[:, None, None, None], result, jnp.zeros_like(result))


def solution(mesh):
    placed = (P("scene", None, None, "strip"), P(), P("scene"), P("scene"), P("scene"))
    return jax.shard_map(
        shards,
        mesh=mesh,
        in_specs=placed,
        out_specs=P("scene", None, None, "strip"),
        check_vma=False,
    )
```

profile of v0, /device:TPU:1, one launch (start us, length us, event | category | flops | bytes accessed | tf_op | source)
XLA Modules:
  0.0 167.5 jit_solution(15226109734729508106)
XLA Ops:
  6.5 0.0 copy-start
  6.5 0.0 all-gather.2.cloned.1.call-start
  6.5 0.7 all-gather.2.cloned.1.call-update
  7.9 0.7 fusion.18
  8.7 0.0 copy-done
  8.7 1.3 gather_fusion
  9.9 101.6 %all-gather.2.cloned.1.call-done = bf16[384,10,2,1024]{3,2,1,0:T(2,128)(2,1)} async-done(((bf16[6,10,2,1024]{3,2,1,0:T(2,128)(2,1)}), bf16[384,10,2,1024]{3,2,1,0:T(2,128)(2,1)}) %all-gather.2.cloned.1.call-update) | async-done | bytes 15728656 | tf_op jit(solution)/shard_map/all_gather | solution.py:24
  111.5 15.7 %fusion.2 = bf16[128,10,2,1024]{3,0,2,1:T(8,128)(2,1)S(1)} fusion(bf16[384,10,2,1024]{3,2,1,0:T(2,128)(2,1)} %all-gather.2.cloned.1.call-done, s32[128]{0:T(128)S(1)} %gather_fusion), kind=kOutput, calls=%fused_computation.12 | convolution fusion | flops 2016034816 | bytes 20972032 | tf_op jit(solution)/shard_map/js,sazr->jazr/dot_general | solution.py:29
  127.2 1.8 %fusion.6 = (f32[64,10,1,1024]{3,0,2,1:T(8,128)S(1)}, f32[64,10,1,1024]{3,0,2,1:T(8,128)S(1)}, f32[64,10,1,1024]{3,0,2,1:T(8,128)S(1)}, f32[64,10,1,1024]{3,0,2,1:T(8,128)S(1)}) fusion(bf16[128,10,2,1024]{3,0,2,1:T(8,128)(2,1)S(1)} %fusion.2), kind=kLoop, calls=%fused_computation.14 | loop fusion | flops 10485760 | bytes 15728640 | tf_op jit(solution)/shard_map/add | solution.py:38
  129.0 1.5 maximum_reduce_fusion
  130.5 0.1 fusion.21
  130.6 3.1 %collective-permute-start = (f32[64,4,2,10]{3,0,2,1:T(8,128)S(1)}, f32[64,4,2,10]{3,0,2,1:T(8,128)S(1)}, u32[]{:S(2)}, u32[]{:S(2)}) collective-permute-start(f32[64,4,2,10]{3,0,2,1:T(8,128)S(1)} %get-tuple-element.10), channel_id=1, source_target_pairs={{0,1},{1,2},{2,3},{4,5},{5,6},{6,7},{8,9},{9,10},{10,11},{12,13},{... | collective-permute-start | bytes 61448 | tf_op jit(solution)/shard_map/ppermute | solution.py:12
  133.8 1.5 collective-permute-start.1
  135.3 3.9 %collective-permute-done = f32[64,4,2,10]{3,0,2,1:T(8,128)S(1)} collective-permute-done((f32[64,4,2,10]{3,0,2,1:T(8,128)S(1)}, f32[64,4,2,10]{3,0,2,1:T(8,128)S(1)}, u32[]{:S(2)}, u32[]{:S(2)}) %collective-permute-start) | collective-permute-done | bytes 20512 | tf_op jit(solution)/shard_map/ppermute | solution.py:12
  139.2 3.8 %collective-permute-done.1 = f32[64,4,2,10]{3,0,2,1:T(8,128)S(1)} collective-permute-done((f32[64,4,2,10]{3,0,2,1:T(8,128)S(1)}, f32[64,4,2,10]{3,0,2,1:T(8,128)S(1)}, u32[]{:S(2)}, u32[]{:S(2)}) %collective-permute-start.1) | collective-permute-done | bytes 20512 | tf_op jit(solution)/shard_map/ppermute | solution.py:15
  143.0 2.6 %concatenate.33 = f32[64,4,2,1044]{3,0,2,1:T(8,128)} concatenate(f32[64,4,2,10]{3,0,2,1:T(8,128)S(1)} %collective-permute-done, f32[64,4,2,1024]{3,0,2,1:T(8,128)S(1)} %maximum_reduce_fusion, f32[64,4,2,10]{3,0,2,1:T(8,128)S(1)} %collective-permute-done.1), dimensions={3} | concatenate | bytes 4276224 | tf_op jit(solution)/shard_map/concatenate | solution.py:16
  145.6 6.9 %copy.9 = f32[64,4,2,1044]{0,2,3,1:T(2,128)} copy(f32[64,4,2,1044]{3,0,2,1:T(8,128)} %concatenate.33) | data formatting | bytes 4276224 | tf_op jit(solution)/shard_map/concatenate | solution.py:16
  152.5 5.4 %reduce_sum.19 = f32[64,4,2,261]{0,2,3,1:T(2,128)S(1)} reduce(f32[64,4,2,261,4]{0,2,4,3,1:T(2,128)} %bitcast.20, f32[]{:T(128)} %constant.2.clone.1), dimensions={4}, to_apply=%region_1.2 | reduce | flops 400896 | bytes 2672644 | tf_op jit(solution)/shard_map/reduce_sum | solution.py:42
  157.9 1.1 slice_add_fusion
  159.1 0.3 fusion.12
  159.4 0.3 maximum_select_fusion
  159.7 0.9 copy.10
  (2 shorter events, 0.0 us)
Async XLA Ops:
  6.5 2.1 %copy-start = (s32[320]{0:T(512)S(1)}, s32[320]{0:T(512)}, u32[]{:S(2)}) copy-start(s32[320]{0:T(512)} %param.6) | copy-start | bytes 3844
  6.5 105.0 %all-gather.2.cloned.1.call-start = ((), (), s32[]{:S(2)}) async-start(), calls=%async_computation | async-start | bytes 15974400 | tf_op jit(solution)/shard_map/all_gather | solution.py:24
  130.6 8.6 %collective-permute-start = (f32[64,4,2,10]{3,0,2,1:T(8,128)S(1)}, f32[64,4,2,10]{3,0,2,1:T(8,128)S(1)}, u32[]{:S(2)}, u32[]{:S(2)}) collective-permute-start(f32[64,4,2,10]{3,0,2,1:T(8,128)S(1)} %get-tuple-element.10), channel_id=1, source_target_pairs={{0,1},{1,2},{2,3},{4,5},{5,6},{6,7},{8,9},{9,10},{10,11},{12,13},{... | collective-permute-start | bytes 61448 | tf_op jit(solution)/shard_map/ppermute | solution.py:12
  133.8 9.2 %collective-permute-start.1 = (f32[64,4,2,10]{3,0,2,1:T(8,128)S(1)}, f32[64,4,2,10]{3,0,2,1:T(8,128)S(1)}, u32[]{:S(2)}, u32[]{:S(2)}) collective-permute-start(f32[64,4,2,10]{3,0,2,1:T(8,128)S(1)} %get-tuple-element.9), channel_id=1, source_target_pairs={{1,0},{2,1},{3,2},{5,4},{6,5},{7,6},{9,8},{10,9},{11,10},{13,12},{... | collective-permute-start | bytes 61448 | tf_op jit(solution)/shard_map/ppermute | solution.py:15
Sparse Core Ops, SparseCore 0:
  10.1 101.3 all-gather.1
where the time goes:
time: 168 us
  waiting for transfers between devices  110 us (65%)
  matrix products  15.7 us (9%)
  between operations  14.1 us (8%)
  local copies, waits for them, and re-layouts  11.8 us (7%)
  other arithmetic  11.2 us (7%)
  starting transfers between devices  4.6 us (3%)
    all_gather x1, waiting for transfers between devices, shards(): piece = lax.all_gather(scene_tiles, 'scene', axis=0, tiled=True)  102 us
    dot_general x1, matrix products, shards(): jnp.einsum('js,sazr->jazr', hit, piece, preferred_element_type=jnp.float32)  15.7 us
    concatenate x2, local copies, waits for them, and re-layouts, extended(): block = jnp.concatenate([low, block, high], axis=dim)  9.5 us
    reduce_sum x1, other arithmetic, shards(): widened.reshape(pcap, 4, lines_az // 5, (range_dev + 20) // 4, 4)  5.41 us
    ppermute x1, waiting for transfers between devices, extended(): lax.ppermute(lax.slice_in_dim(block, block.shape[dim] - width, None, axis...  3.94 us
    ppermute x1, waiting for transfers between devices, extended(): lax.ppermute(lax.slice_in_dim(block, 0, width, axis=dim), axis, backward)  3.81 us
  transfers between devices with their start and end apart: 3, of which 3 were waited for; matrix products, arithmetic and copies ran while one was open for 1% of the time, Pallas kernels for 0%

commit v1 on v0

v1 whole, which is shorter than its diff:
```python
import functools

import jax
import jax.numpy as jnp
import numpy as np
from jax import lax
from jax.experimental import pallas as pl
from jax.experimental.pallas import tpu as pltpu
from jax.sharding import PartitionSpec as P

MESH = pl.DeviceIdType.MESH
F32 = jnp.float32
BF16 = jnp.bfloat16

XS, ZS, CHIPS = 4, 8, 32
STRIPS = 4
SLOTS = 6
AZ = 5
TILES = 8
ROWS = 480


def feature_order():
    order = np.zeros((ROWS, 512), np.float32)
    for az in range(AZ):
        for ri in range(2):
            for cell in range(-10, 38):
                block, w = (cell + 2) // 4, (cell + 2) % 4
                base = 96 * az + 48 * ri
                if 0 <= block < 8:
                    row = base + 8 * w + block
                else:
                    row = base + 32 + 4 * w + {-2: 0, -1: 1, 8: 2, 9: 3}[block]
                if 0 <= cell < 32:
                    lane = 32 * (2 * az + ri) + cell
                else:
                    h = cell + 10 if cell < 0 else cell - 22
                    lane = 32 * (10 + az) + 16 * ri + h
                order[row, lane] = 1.0
    return order


def far_first(i):
    return jnp.where(i == 0, 2, jnp.where(i == 1, 1, jnp.where(i == 2, 3, 0)))


def windows(main, halo):
    row = lax.broadcasted_iota(jnp.int32, main.shape, 0)
    total = main + jnp.where(row < 1, pltpu.roll(halo, 7, 0), pltpu.roll(main, 1, 0))
    total += jnp.where(row < 2, halo, pltpu.roll(main, 2, 0))
    total += jnp.where(row >= 7, pltpu.roll(halo, 1, 0), pltpu.roll(main, 7, 0))
    total += jnp.where(row >= 6, halo, pltpu.roll(main, 6, 0))
    return total


def kernel(
    tiles_ref, slot_ref, list_ref, order_ref, out_ref,
    ext, msg, land, lst, chip_list, lists, scene_k, hot, feat, both, res, back, turned, fin,
    own_sem, core_send, core_recv, edge_send, edge_recv, list_send, list_recv,
    data_send, data_recv, back_send, back_recv,
):
    me = lax.axis_index("scene")
    y = lax.axis_index("strip")
    chip, c = me // 2, lax.rem(me, 2)
    other = 1 - c
    x, z = chip // ZS, lax.rem(chip, ZS)
    up, down = lax.rem(y + 1, STRIPS), lax.rem(y + STRIPS - 1, STRIPS)
    partner = {"scene": chip * 2 + other}

    barrier = pltpu.get_barrier_semaphore()

    def greet(k, carry):
        @pl.when(k != chip)
        def _():
            pl.semaphore_signal(barrier, inc=1, device_id={"scene": 2 * k + c}, device_id_type=MESH)
        return carry

    lax.fori_loop(0, CHIPS, greet, 0)
    pl.semaphore_signal(barrier, inc=1, device_id=partner, device_id_type=MESH)
    for row in (up, down):
        for core in (c, other):
            pl.semaphore_signal(
                barrier, inc=1, device_id={"scene": chip * 2 + core, "strip": row}, device_id_type=MESH
            )

    own = pltpu.make_async_copy(tiles_ref.at[c], ext.at[c, :, :, pl.ds(128, 1024)], own_sem)
    own.start()

    rows = lax.broadcasted_iota(jnp.int32, (512, 384), 0)
    place = lax.rem(rows, 8)
    slot = (rows // 16) * 12 + (lax.rem(rows, 16) // 8) * 6 + place
    slot = jnp.where(place < SLOTS, slot, -7)
    lane = lax.broadcasted_iota(jnp.int32, (512, 384), 1).astype(F32)
    scene = jnp.sum(jnp.where(slot == slot_ref[...], lane + 1.0, 0.0), axis=1, keepdims=True) - 1.0
    scene_k[...] = jnp.broadcast_to(scene, (512, 128)).astype(jnp.int32)

    pl.semaphore_wait(barrier, CHIPS - 1 + 1 + 4)

    give_list = pltpu.make_async_remote_copy(
        src_ref=list_ref, dst_ref=lst, send_sem=core_send.at[0], recv_sem=core_recv.at[0],
        device_id=partner, device_id_type=MESH,
    )
    give_list.start()
    give_line = pltpu.make_async_remote_copy(
        src_ref=tiles_ref.at[other], dst_ref=ext.at[c, :, :, pl.ds(128, 1024)],
        send_sem=core_send.at[1], recv_sem=core_recv.at[1], device_id=partner, device_id_type=MESH,
    )
    give_line.start()
    edges = []
    for side, (row, src, dst) in enumerate(((up, 896, 0), (down, 0, 1152))):
        for n, core in enumerate((c, other)):
            copy = pltpu.make_async_remote_copy(
                src_ref=tiles_ref.at[core, :, :, pl.ds(src, 128)],
                dst_ref=ext.at[c, :, :, pl.ds(dst, 128)],
                send_sem=edge_send.at[2 * side + n],
                recv_sem=edge_recv.at[2 * side + n],
                device_id={"scene": chip * 2 + core, "strip": row},
                device_id_type=MESH,
            )
            copy.start()
            edges.append(copy)

    give_list.wait()
    half = lax.broadcasted_iota(jnp.int32, (2, 128), 1) // 64
    chip_list[...] = jnp.where(half == c, list_ref[...], lst[...])
    lists[chip] = chip_list[...]

    def list_copy(k):
        return pltpu.make_async_remote_copy(
            src_ref=chip_list, dst_ref=lists.at[chip], send_sem=list_send.at[k], recv_sem=list_recv.at[chip],
            device_id={"scene": 2 * k + c}, device_id_type=MESH,
        )

    def send_list(i, carry):
        k = lax.rem(x + far_first(i // ZS), XS) * ZS + lax.rem(z + 4 + i, ZS)

        @pl.when(k != chip)
        def _():
            list_copy(k).start()
        return carry

    lax.fori_loop(0, CHIPS, send_list, 0)

    own.wait()
    give_line.wait()
    for copy in edges:
        copy.wait()

    @pl.when(y == 0)
    def _():
        ext[:, :, :, 0:128] = jnp.zeros((2, AZ, 16, 128), BF16)

    @pl.when(y == STRIPS - 1)
    def _():
        ext[:, :, :, 1152:1280] = jnp.zeros((2, AZ, 16, 128), BF16)

    lanes = lax.broadcasted_iota(jnp.int32, (16, 128), 1)
    in32 = lax.rem(lanes, 32)
    row8 = lax.broadcasted_iota(jnp.int32, (2, 8, 128), 1)

    def data_copy(k):
        return pltpu.make_async_remote_copy(
            src_ref=msg.at[k], dst_ref=land.at[chip], send_sem=data_send.at[k], recv_sem=data_recv.at[chip],
            device_id={"scene": 2 * k + c}, device_id_type=MESH,
        )

    def pack(i, carry):
        first = 1 - z // 4
        h = jnp.where(lax.rem(i, 2) == 0, first, 1 - first)
        t = lax.rem(x + far_first(i // 2), XS) * 2 + h
        at = pl.ds(pl.multiple_of(t * 128, 128), 384)
        groups, halos = [], []
        for az in range(AZ):
            v = [ext[core, az, :, at].astype(F32) for core in range(2)]
            re = jnp.concatenate([v[0][0:8], v[1][0:8]], axis=0)
            im = jnp.concatenate([v[0][8:16], v[1][8:16]], axis=0)
            groups += [re[:, 128:256], im[:, 128:256]]
            near = jnp.where(in32 < 10, pltpu.roll(re, 10, 1)[:, 128:256], pltpu.roll(re, 384 - 22, 1)[:, 128:256])
            far = jnp.where(in32 < 26, pltpu.roll(im, 26, 1)[:, 128:256], pltpu.roll(im, 384 - 6, 1)[:, 128:256])
            halos.append(jnp.where(in32 < 16, near, far))
        groups += halos + [jnp.zeros((16, 128), F32)]
        turned4 = []
        for s in range(4):
            g = groups[4 * s : 4 * s + 4]
            low = lanes < 64
            for a, b in ((0, 2), (1, 3)):
                ga, gb = g[a], g[b]
                g[a] = jnp.where(low, ga, pltpu.roll(gb, 64, 1))
                g[b] = jnp.where(low, pltpu.roll(ga, 64, 1), gb)
            low = lax.rem(lanes, 64) < 32
            for a, b in ((0, 1), (2, 3)):
                ga, gb = g[a], g[b]
                g[a] = jnp.where(low, ga, pltpu.roll(gb, 32, 1))
                g[b] = jnp.where(low, pltpu.roll(ga, 96, 1), gb)
            turned4.append(g)
        for sub in range(4):
            k = 4 * t + sub
            last = turned4[3][sub].reshape(2, 8, 128)
            for s in range(3):
                tile = turned4[s][sub].reshape(2, 8, 128)
                tile = jnp.where(row8 >= 6, pltpu.roll(last, 6 - 2 * s, 1), tile)
                msg[k, :, 128 * s : 128 * s + 128] = tile.reshape(16, 128).astype(BF16)

            @pl.when(k != chip)
            def _():
                data_copy(k).start()
        return carry

    lax.fori_loop(0, TILES, pack, 0)
    land[chip] = msg[chip]

    def get_list(k, carry):
        @pl.when(k != chip)
        def _():
            pltpu.make_async_remote_copy(
                src_ref=chip_list, dst_ref=lists.at[k], send_sem=list_send.at[k], recv_sem=list_recv.at[k],
                device_id={"scene": 2 * k + c}, device_id_type=MESH,
            ).wait()
        return carry

    lax.fori_loop(0, CHIPS, get_list, 0)

    def one_hot(m, carry):
        for n in range(2):
            pair = lists[2 * m + n]
            for part in range(2):
                hit = jnp.where(scene_k[...] == pair[part : part + 1, :], 1.0, 0.0).astype(BF16)
                hot[m, :, 256 * part + 128 * n : 256 * part + 128 * n + 128] = hit
        return carry

    lax.fori_loop(0, CHIPS // 2, one_hot, 0)

    def get_data(k, carry):
        @pl.when(k != chip)
        def _():
            pltpu.make_async_remote_copy(
                src_ref=msg.at[k], dst_ref=land.at[k], send_sem=data_send.at[k], recv_sem=data_recv.at[k],
                device_id={"scene": 2 * k + c}, device_id_type=MESH,
            ).wait()
        return carry

    lax.fori_loop(0, CHIPS, get_data, 0)

    part = [land[:, :, 128 * s : 128 * s + 128].reshape(512, 128) for s in range(3)]
    wide = [p.astype(F32).reshape(64, 8, 128) for p in part]
    row = lax.broadcasted_iota(jnp.int32, (64, 8, 128), 1)
    last = jnp.where(
        row < 2, pltpu.roll(wide[0], 2, 1), jnp.where(row < 4, pltpu.roll(wide[1], 4, 1), pltpu.roll(wide[2], 6, 1))
    )
    sent = jnp.concatenate(part + [last.reshape(512, 128).astype(BF16)], axis=1)
    feat[...] = lax.dot_general(
        order_ref[...], sent, (((1,), (1,)), ((), ())), preferred_element_type=F32
    ).astype(BF16)

    def back_copy(k):
        return pltpu.make_async_remote_copy(
            src_ref=res.at[k], dst_ref=back.at[chip], send_sem=back_send.at[k], recv_sem=back_recv.at[chip],
            device_id={"scene": 2 * k + c}, device_id_type=MESH,
        )

    def compute(i, carry):
        zp = lax.rem(z // 2 + far_first(lax.rem(i, 4)), 4)
        m = lax.rem(x + far_first(i // 4), XS) * 4 + zp
        both[...] = jnp.dot(feat[...], hot[m], preferred_element_type=F32)
        main, halo = [0.0] * 4, [0.0] * 4
        for az in range(AZ):
            a0, b0 = both[96 * az : 96 * az + 48, 0:256], both[96 * az : 96 * az + 48, 256:512]
            a1, b1 = both[96 * az + 48 : 96 * az + 96, 0:256], both[96 * az + 48 : 96 * az + 96, 256:512]
            planes = (a0 * b0 + a1 * b1, a1 * b0 - a0 * b1, a0 * a0 + a1 * a1, b0 * b0 + b1 * b1)
            for n, plane in enumerate(planes):
                for w in range(4):
                    main[n] = main[n] + plane[8 * w : 8 * w + 8]
                for w in range(4, 6):
                    halo[n] = halo[n] + plane[8 * w : 8 * w + 8]
        looks = [windows(u, v + pltpu.roll(v, 4, 0)) for u, v in zip(main, halo)]
        scale = lax.rsqrt(looks[2] * looks[3] + 1e-06)
        value = jnp.concatenate([looks[0] * scale, looks[1] * scale], axis=0)
        for n in range(2):
            k = 2 * m + n
            res[k] = value[:, 128 * n : 128 * n + 128]

            @pl.when(k != chip)
            def _():
                back_copy(k).start()
        return carry

    lax.fori_loop(0, CHIPS // 2, compute, 0)
    back[chip] = res[chip]

    def get_back(k, carry):
        @pl.when(k != chip)
        def _():
            pltpu.make_async_remote_copy(
                src_ref=res.at[k], dst_ref=back.at[k], send_sem=back_send.at[k], recv_sem=back_recv.at[k],
                device_id={"scene": 2 * k + c}, device_id_type=MESH,
            ).wait()
        return carry

    lax.fori_loop(0, CHIPS, get_back, 0)

    for ri in range(2):
        turned[ri] = back[:, 8 * ri : 8 * ri + 8, :].reshape(256, 128).T
    give = pltpu.make_async_remote_copy(
        src_ref=turned.at[:, pl.ds(pl.multiple_of(64 * other, 64), 64), :], dst_ref=fin,
        send_sem=core_send.at[2], recv_sem=core_recv.at[2], device_id=partner, device_id_type=MESH,
    )
    give.start()
    out_ref[c] = turned[:, pl.ds(pl.multiple_of(64 * c, 64), 64), :]
    give.wait()
    out_ref[other] = fin[...]


def shards(scene_tiles, scene_slot, pair_ref, pair_sec, pair_count):
    pcap = pair_ref.shape[0]
    tiles = jnp.pad(scene_tiles, ((0, 2), (0, 0), (0, 0), (0, 0)))
    tiles = tiles.reshape(8, 2, AZ, 2, 1024).transpose(1, 2, 3, 0, 4).reshape(2, AZ, 16, 1024)
    slots = jnp.pad(scene_slot, (0, 64), constant_values=-9).reshape(1, 384)
    live = jnp.arange(pcap, dtype=jnp.int32) < pair_count[0]
    pairs = jnp.where(live, jnp.stack([pair_ref, pair_sec]), -2)
    pairs = jnp.concatenate([pairs, pairs], axis=1)
    order = jnp.asarray(feature_order(), BF16)
    vmem = pl.BlockSpec(memory_space=pltpu.VMEM)
    dma = pltpu.SemaphoreType.DMA
    out = pl.pallas_call(
        kernel,
        out_shape=jax.ShapeDtypeStruct((2, 2, pcap, 256), F32),
        in_specs=[vmem] * 4,
        out_specs=vmem,
        scratch_shapes=[
            pltpu.VMEM((2, AZ, 16, 1280), BF16),
            pltpu.VMEM((CHIPS, 16, 384), BF16),
            pltpu.VMEM((CHIPS, 16, 384), BF16),
            pltpu.VMEM((2, 128), jnp.int32),
            pltpu.VMEM((2, 128), jnp.int32),
            pltpu.VMEM((CHIPS, 2, 128), jnp.int32),
            pltpu.VMEM((512, 128), jnp.int32),
            pltpu.VMEM((CHIPS // 2, 512, 512), BF16),
            pltpu.VMEM((ROWS, 512), BF16),
            pltpu.VMEM((ROWS, 512), F32),
            pltpu.VMEM((CHIPS, 16, 128), F32),
            pltpu.VMEM((CHIPS, 16, 128), F32),
            pltpu.VMEM((2, 128, 256), F32),
            pltpu.VMEM((2, 64, 256), F32),
            dma, dma((3,)), dma((3,)), dma((4,)), dma((4,)), dma((CHIPS,)), dma((CHIPS,)),
            dma((CHIPS,)), dma((CHIPS,)), dma((CHIPS,)), dma((CHIPS,)),
        ],
        compiler_params=pltpu.CompilerParams(
            collective_id=0, has_side_effects=True, vmem_limit_bytes=48 << 20
        ),
        name="coherence",
    )(tiles, slots, pairs, order)
    return out.transpose(2, 0, 1, 3)


def solution(mesh):
    placed = (P("scene", None, None, "strip"), P(), P("scene"), P("scene"), P("scene"))
    return jax.shard_map(
        shards,
        mesh=mesh,
        in_specs=placed,
        out_specs=P("scene", None, None, "strip"),
        check_vma=False,
    )
```

time: 168 us -> 47.2 us (0.28)
  waiting for transfers between devices: 110 us -> 0 us
  Pallas kernels: 0 us -> 42.8 us
  matrix products: 15.7 us -> 0 us
  between operations: 14.1 us -> 0.71 us
  other arithmetic: 11.2 us -> 0.09 us
  local copies, waits for them, and re-layouts: 11.8 us -> 3.48 us
  starting transfers between devices: 4.6 us -> 0 us
    all_gather x1 -> x0, waiting for transfers between devices: 102 us -> none  [shards(): piece = lax.all_gather(scene_tiles, 'scene', axis=0, tiled=True)]
    pallas_call x0 -> x1, Pallas kernels: none -> 42.8 us  [shards(): pl.pallas_call(kernel, out_shape=jax.ShapeDtypeStruct((2, 2, pcap, 256),...]
    dot_general x1 -> x0, matrix products: 15.7 us -> none  [shards(): jnp.einsum('js,sazr->jazr', hit, piece, preferred_element_type=jnp.float32)]
    concatenate x2 -> x0, local copies, waits for them, and re-layouts: 9.5 us -> none  [extended(): block = jnp.concatenate([low, block, high], axis=dim)]
    ppermute x2 -> x0, waiting for transfers between devices: 7.74 us -> none  [the longest x1 3.94 us: extended(): lax.ppermute(lax.slice_in_dim(block, block.shape[dim] - width, None, axis...]
    reduce_sum x2 -> x0, other arithmetic: 6.88 us -> none  [the longest x1 5.41 us: shards(): widened.reshape(pcap, 4, lines_az // 5, (range_dev + 20) // 4, 4)]
    ppermute x2 -> x0, starting transfers between devices: 4.6 us -> none  [the longest x1 3.12 us: extended(): lax.ppermute(lax.slice_in_dim(block, block.shape[dim] - width, None, axis...]
    add x2 -> x0, other arithmetic: 2.91 us -> none  [the longest x1 1.77 us: shards(): a0 * b0 + a1 * b1]
  transfers between devices with their start and end apart: 3 -> 0, of which waited for: 3 -> 0; matrix products, arithmetic and copies ran while one was open for 1% -> 0% of each run, Pallas kernels for 0% -> 0%
where the time goes in v1:
time: 47.2 us; the launch traced here: 47 us
  Pallas kernels  42.8 us (91%)
  local copies, waits for them, and re-layouts  3.48 us (7%)
  between operations  0.71 us (2%)
    pallas_call x1, Pallas kernels, shards(): pl.pallas_call(kernel, out_shape=jax.ShapeDtypeStruct((2, 2, pcap, 256),...  42.8 us
    pad x1, local copies, waits for them, and re-layouts, shards(): tiles = jnp.pad(scene_tiles, ((0, 2), (0, 0), (0, 0), (0, 0)))  1.23 us
    unnamed x8, local copies, waits for them, and re-layouts  1.23 us

profile of v1, /device:TPU:1, one launch (start us, length us, event | category | flops | bytes accessed | tf_op | source)
XLA Modules:
  0.0 47.0 jit_solution(7146640130235511481)
XLA Ops:
  0.0 0.0 copy-start
  0.0 1.2 %pad.8 = bf16[8,10,2,1024]{3,2,1,0:T(2,128)(2,1)S(1)} pad(bf16[6,10,2,1024]{3,2,1,0:T(2,128)(2,1)} %param.6, bf16[]{:T(256)} %constant.2.clone.1), padding=0_2x0_0x0_0x0_0 | pad | bytes 573442 | tf_op jit(solution)/shard_map/jit(_pad)/pad | solution.py:315
  1.2 0.0 copy-start.1
  1.2 0.1 copy.10
  1.4 0.6 %copy-done.1 = s32[320]{0:T(512)S(1)} copy-done((s32[320]{0:T(512)S(1)}, s32[320]{0:T(512)}, u32[]{:S(2)}) %copy-start.1) | copy-done | bytes 1304
  2.6 0.0 copy-start.2
  2.6 0.0 copy-start.3
  2.6 0.6 %copy-done.2 = s32[64]{0:T(128)S(1)} copy-done((s32[64]{0:T(128)S(1)}, s32[64]{0:T(128)}, u32[]{:S(2)}) %copy-start.2) | copy-done | bytes 280
  3.3 0.0 copy-done.3
  3.3 0.1 pad_add_fusion.list_ref
  3.4 0.0 copy-done
  3.4 42.8 %coherence.1 = f32[2,2,64,256]{3,2,1,0:T(8,128)S(1)} custom-call(bf16[2,5,16,1024]{3,2,1,0:T(8,128)(2,1)S(1)} %bitcast.11, s32[1,384]{1,0:T(1,128)S(1)} %reshape.11.slot_ref, s32[2,128]{1,0:T(2,128)S(1)} %pad_add_fusion.list_ref, bf16[480,512]{1,0:T(8,128)(2,1)S(1)} %copy-done), custom_call_target="tpu_custom_call" | custom-call | tf_op jit(solution)/shard_map/coherence/pallas_call | solution.py:324
  46.1 0.9 %copy.8 = f32[64,2,2,256]{3,2,1,0:T(2,128)} copy(f32[64,2,2,256]{3,0,2,1:T(8,128)S(1)} %bitcast.12) | data formatting | bytes 524288 | tf_op jit(solution)/shard_map/transpose | solution.py:352
  (4 shorter events, 0.0 us)
Async XLA Ops:
  0.0 3.4 %copy-start = (bf16[480,512]{1,0:T(8,128)(2,1)S(1)}, bf16[480,512]{1,0:T(8,128)(2,1)}, u32[]{:S(2)}) copy-start(bf16[480,512]{1,0:T(8,128)(2,1)} %constant.9.clone.order_ref) | copy-start | bytes 1474564
  1.2 0.7 %copy-start.1 = (s32[320]{0:T(512)S(1)}, s32[320]{0:T(512)}, u32[]{:S(2)}) copy-start(s32[320]{0:T(512)} %param.7) | copy-start | bytes 3844
  2.6 0.7 %copy-start.2 = (s32[64]{0:T(128)S(1)}, s32[64]{0:T(128)}, u32[]{:S(2)}) copy-start(s32[64]{0:T(128)} %param.9) | copy-start | bytes 772
  2.6 0.7 %copy-start.3 = (s32[64]{0:T(128)S(1)}, s32[64]{0:T(128)}, u32[]{:S(2)}) copy-start(s32[64]{0:T(128)} %param.8) | copy-start | bytes 772

commit v2 on v1

v2 whole, which is shorter than its diff:
```python
import functools

import jax
import jax.numpy as jnp
import numpy as np
from jax import lax
from jax.experimental import pallas as pl
from jax.experimental.pallas import tpu as pltpu
from jax.sharding import PartitionSpec as P

MESH = pl.DeviceIdType.MESH
F32 = jnp.float32
BF16 = jnp.bfloat16

XS, ZS, CHIPS = 4, 8, 32
STRIPS = 4
SLOTS = 6
AZ = 5
TILES = 8
ROWS = 480


def feature_order():
    order = np.zeros((ROWS, 512), np.float32)
    for az in range(AZ):
        for ri in range(2):
            for cell in range(-10, 38):
                block, w = (cell + 2) // 4, (cell + 2) % 4
                base = 96 * az + 48 * ri
                if 0 <= block < 8:
                    row = base + 8 * w + block
                else:
                    row = base + 32 + 4 * w + {-2: 0, -1: 1, 8: 2, 9: 3}[block]
                if 0 <= cell < 32:
                    lane = 32 * (2 * az + ri) + cell
                else:
                    h = cell + 10 if cell < 0 else cell - 22
                    lane = 32 * (10 + az) + 16 * ri + h
                order[row, lane] = 1.0
    return order


def far_first(i):
    return jnp.where(i == 0, 2, jnp.where(i == 1, 1, jnp.where(i == 2, 3, 0)))


def across(x, i):
    low = lax.rem(x, 2)
    high = x // 2
    flip = jnp.where(lax.rem(i, 3) == 0, low, 1 - low)
    return jnp.where(i < 2, 1 - high, high) * 2 + flip


def both_parts(v):
    rows = jnp.zeros((2, v.shape[-1]), F32)
    v = v.astype(F32)
    return jnp.concatenate([v[:, 0, :], rows, v[:, 1, :], rows], axis=0).astype(BF16)


def windows(main, halo):
    row = lax.broadcasted_iota(jnp.int32, main.shape, 0)
    total = main + jnp.where(row < 1, pltpu.roll(halo, 7, 0), pltpu.roll(main, 1, 0))
    total += jnp.where(row < 2, halo, pltpu.roll(main, 2, 0))
    total += jnp.where(row >= 7, pltpu.roll(halo, 1, 0), pltpu.roll(main, 7, 0))
    total += jnp.where(row >= 6, halo, pltpu.roll(main, 6, 0))
    return total


def kernel(
    tiles_hbm, slot_hbm, ref_hbm, sec_hbm, count_hbm, order_hbm, out_ref,
    slot_ref, ref_ref, sec_ref, count_ref, order_ref, raw, pre, ext, edge, edge_msg, sent, msg, land, own_list, lst, chip_list, lists, scene_k, hot, feat, both_a, both_b,
    res, back, turned, fin,
    in_sem, core_send, core_recv, edge_send, edge_recv, list_send, list_recv,
    data_send, data_recv, back_send, back_recv, fin_send, fin_recv,
):
    me = lax.axis_index("scene")
    y = lax.axis_index("strip")
    chip, c = me // 2, lax.rem(me, 2)
    other = 1 - c
    x, z = chip // ZS, lax.rem(chip, ZS)
    partner = {"scene": chip * 2 + other}

    barrier = pltpu.get_barrier_semaphore()

    def greet(k, carry):
        @pl.when(k != chip)
        def _():
            pl.semaphore_signal(barrier, inc=1, device_id={"scene": 2 * k + c}, device_id_type=MESH)
        return carry

    pl.semaphore_signal(barrier, inc=1, device_id=partner, device_id_type=MESH)
    lax.fori_loop(0, CHIPS, greet, 0)

    at_left = (chip == 0) & (y > 0)
    at_right = (chip == CHIPS - 1) & (y < STRIPS - 1)
    side = jnp.where(chip == 0, y - 1, y + 1)

    def greet_side(k, carry):
        pl.semaphore_signal(
            barrier, inc=1, device_id={"scene": 2 * k + c, "strip": side}, device_id_type=MESH
        )
        return carry

    @pl.when(at_left | at_right)
    def _():
        lax.fori_loop(0, CHIPS, greet_side, 0)

    gets = [
        pltpu.make_async_copy(src, dst, in_sem.at[n])
        for n, (src, dst) in enumerate((
            (tiles_hbm, raw), (ref_hbm, ref_ref), (sec_hbm, sec_ref), (count_hbm, count_ref),
            (slot_hbm, slot_ref), (order_hbm, order_ref),
        ))
    ]
    for get in gets:
        get.start()
    for get in gets[1:4]:
        get.wait()
    mine = lax.broadcasted_iota(jnp.int32, (1, 64), 1) < count_ref[...]
    for n, ref in enumerate((ref_ref, sec_ref)):
        pair = jnp.where(mine, ref[...], -2)
        own_list[n : n + 1, 0:64] = pair
        own_list[n : n + 1, 64:128] = pair
    ext[:, :, :, 0:128] = jnp.zeros((2, AZ, 16, 128), BF16)
    ext[:, :, :, 1152:1280] = jnp.zeros((2, AZ, 16, 128), BF16)
    gets[0].wait()

    def lines(az, carry):
        pre[az] = both_parts(raw[:, 5 * other + az])
        ext[c, az, :, 128:1152] = both_parts(raw[:, 5 * c + az])
        return carry

    lax.fori_loop(0, AZ, lines, 0)
    sides = jnp.where(y < STRIPS - 1, 1, 0) + jnp.where(y > 0, 1, 0)
    pl.semaphore_wait(barrier, CHIPS + sides)

    give_line = pltpu.make_async_remote_copy(
        src_ref=pre, dst_ref=ext.at[c, :, :, pl.ds(128, 1024)],
        send_sem=core_send.at[1], recv_sem=core_recv.at[1], device_id=partner, device_id_type=MESH,
    )
    give_line.start()
    give_list = pltpu.make_async_remote_copy(
        src_ref=own_list, dst_ref=lst, send_sem=core_send.at[0], recv_sem=core_recv.at[0],
        device_id=partner, device_id_type=MESH,
    )
    give_list.start()

    give_list.wait()
    half = lax.broadcasted_iota(jnp.int32, (2, 128), 1) // 64
    chip_list[...] = jnp.where(half == c, own_list[...], lst[...])
    lists[chip] = chip_list[...]

    def list_copy(k):
        return pltpu.make_async_remote_copy(
            src_ref=chip_list, dst_ref=lists.at[chip], send_sem=list_send.at[k], recv_sem=list_recv.at[chip],
            device_id={"scene": 2 * k + c}, device_id_type=MESH,
        )

    def send_list(i, carry):
        k = across(x, i // ZS) * ZS + lax.rem(z + 4 + i, ZS)

        @pl.when(k != chip)
        def _():
            list_copy(k).start()
        return carry

    give_line.wait()

    lanes = lax.broadcasted_iota(jnp.int32, (16, 128), 1)
    in32 = lax.rem(lanes, 32)
    row8 = lax.broadcasted_iota(jnp.int32, (2, 8, 128), 1)

    def data_copy(k):
        return pltpu.make_async_remote_copy(
            src_ref=msg.at[k], dst_ref=land.at[chip], send_sem=data_send.at[k], recv_sem=data_recv.at[chip],
            device_id={"scene": 2 * k + c}, device_id_type=MESH,
        )

    def pack(t):
        at = pl.ds(pl.multiple_of(t * 128, 128), 384)
        groups, halos = [], []
        for az in range(AZ):
            v = [ext[core, az, :, at].astype(F32) for core in range(2)]
            re = jnp.concatenate([v[0][0:8], v[1][0:8]], axis=0)
            im = jnp.concatenate([v[0][8:16], v[1][8:16]], axis=0)
            groups += [re[:, 128:256], im[:, 128:256]]
            near = jnp.where(in32 < 10, pltpu.roll(re, 10, 1)[:, 128:256], pltpu.roll(re, 384 - 22, 1)[:, 128:256])
            far = jnp.where(in32 < 26, pltpu.roll(im, 26, 1)[:, 128:256], pltpu.roll(im, 384 - 6, 1)[:, 128:256])
            halos.append(jnp.where(in32 < 16, near, far))
        groups += halos + [jnp.zeros((16, 128), F32)]
        turned4 = []
        for s in range(4):
            g = groups[4 * s : 4 * s + 4]
            low = lanes < 64
            for a, b in ((0, 2), (1, 3)):
                ga, gb = g[a], g[b]
                g[a] = jnp.where(low, ga, pltpu.roll(gb, 64, 1))
                g[b] = jnp.where(low, pltpu.roll(ga, 64, 1), gb)
            low = lax.rem(lanes, 64) < 32
            for a, b in ((0, 1), (2, 3)):
                ga, gb = g[a], g[b]
                g[a] = jnp.where(low, ga, pltpu.roll(gb, 32, 1))
                g[b] = jnp.where(low, pltpu.roll(ga, 96, 1), gb)
            turned4.append(g)
        for sub in range(4):
            k = 4 * t + sub
            last = turned4[3][sub].reshape(2, 8, 128)
            for s in range(3):
                tile = turned4[s][sub].reshape(2, 8, 128)
                tile = jnp.where(row8 >= 6, pltpu.roll(last, 6 - 2 * s, 1), tile)
                msg[k, :, 128 * s : 128 * s + 128] = tile.reshape(16, 128).astype(BF16)
        for sub in range(4):
            k = 4 * t + sub

            @pl.when(k != chip)
            def _():
                data_copy(k).start()

    def tile_at(i):
        first = 1 - z // 4
        return across(x, i // 2) * 2 + jnp.where(lax.rem(i, 2) == 0, first, 1 - first)

    def pack_at(i, carry):
        pack(tile_at(i))
        return carry

    def edge_pack(n, start):
        whole = jnp.zeros((16, 128), F32)
        for az in range(AZ):
            v = [ext[core, az, :, start : start + 128].astype(F32) for core in range(2)]
            re = jnp.concatenate([v[0][0:8], v[1][0:8]], axis=0)
            im = jnp.concatenate([v[0][8:16], v[1][8:16]], axis=0)
            for s in range(3 if az == 4 else 1):
                to = 32 * s if az == 4 else 32 * ((az + 2) % 4)
                here = jnp.where(in32 < 16, pltpu.roll(re, 10 + to, 1), pltpu.roll(im, (26 + to) % 128, 1))
                if az == 4:
                    here = pltpu.roll(here.reshape(2, 8, 128), 6 - 2 * s, 1).reshape(16, 128)
                    keep = (lanes // 32 == s) & (row8.reshape(16, 128) >= 6)
                else:
                    keep = lanes // 32 == to // 32
                whole = jnp.where(keep, here, whole)
        edge_msg[n] = whole.astype(BF16)

    def edge_copy(n, to, row):
        return pltpu.make_async_remote_copy(
            src_ref=edge_msg.at[n], dst_ref=edge.at[chip], send_sem=edge_send.at[n], recv_sem=edge_recv.at[chip],
            device_id={"scene": 2 * to + c, "strip": row}, device_id_type=MESH,
        )

    pack_at(0, 0)
    edge_pack(0, 1024)
    edge_pack(1, 128)

    @pl.when(y < STRIPS - 1)
    def _():
        edge_copy(0, 0, y + 1).start()

    @pl.when(y > 0)
    def _():
        edge_copy(1, CHIPS - 1, y - 1).start()

    lax.fori_loop(1, 3, pack_at, 0)
    lax.fori_loop(0, CHIPS, send_list, 0)
    lax.fori_loop(3, TILES, pack_at, 0)

    @pl.when(y < STRIPS - 1)
    def _():
        edge_copy(0, 0, y + 1).wait_send()

    @pl.when(y > 0)
    def _():
        edge_copy(1, CHIPS - 1, y - 1).wait_send()

    land[chip] = msg[chip]

    gets[4].wait()
    gets[5].wait()

    rows = lax.broadcasted_iota(jnp.int32, (512, 320), 0)
    place = lax.rem(rows, 8)
    slot = (rows // 16) * 12 + (lax.rem(rows, 16) // 8) * 6 + place
    slot = jnp.where(place < SLOTS, slot, -7)
    lane = lax.broadcasted_iota(jnp.int32, (512, 320), 1).astype(F32)
    scene = jnp.sum(jnp.where(slot == slot_ref[...].reshape(1, 320), lane + 1.0, 0.0), axis=1, keepdims=True) - 1.0
    scene_k[...] = jnp.broadcast_to(scene, (512, 128)).astype(jnp.int32)

    def get_list(k, carry):
        @pl.when(k != chip)
        def _():
            pltpu.make_async_remote_copy(
                src_ref=chip_list, dst_ref=lists.at[k], send_sem=list_send.at[k], recv_sem=list_recv.at[k],
                device_id={"scene": 2 * k + c}, device_id_type=MESH,
            ).wait()
        return carry

    lax.fori_loop(0, CHIPS, get_list, 0)

    def one_hot(m, carry):
        for n in range(2):
            pair = lists[2 * m + n]
            for part in range(2):
                hit = jnp.where(scene_k[...] == pair[part : part + 1, :], 1.0, 0.0).astype(BF16)
                hot[m, :, 256 * part + 128 * n : 256 * part + 128 * n + 128] = hit
        return carry

    lax.fori_loop(0, CHIPS // 2, one_hot, 0)

    def get_data(k, carry):
        @pl.when(k != chip)
        def _():
            pltpu.make_async_remote_copy(
                src_ref=msg.at[k], dst_ref=land.at[k], send_sem=data_send.at[k], recv_sem=data_recv.at[k],
                device_id={"scene": 2 * k + c}, device_id_type=MESH,
            ).wait()
        return carry

    lax.fori_loop(0, CHIPS, get_data, 0)

    part = [land[:, :, 128 * s : 128 * s + 128].reshape(512, 128) for s in range(3)]
    wide = [p.astype(F32).reshape(64, 8, 128) for p in part]
    row = lax.broadcasted_iota(jnp.int32, (64, 8, 128), 1)
    last = jnp.where(
        row < 2, pltpu.roll(wide[0], 2, 1), jnp.where(row < 4, pltpu.roll(wide[1], 4, 1), pltpu.roll(wide[2], 6, 1))
    )
    sent[...] = jnp.concatenate(part + [last.reshape(512, 128).astype(BF16)], axis=1)

    def get_edge(k, carry):
        pltpu.make_async_remote_copy(
            src_ref=edge_msg.at[0], dst_ref=edge.at[k], send_sem=edge_send.at[0], recv_sem=edge_recv.at[k],
            device_id={"scene": 2 * k + c, "strip": side}, device_id_type=MESH,
        ).wait_recv()
        return carry

    @pl.when(at_left | at_right)
    def _():
        lax.fori_loop(0, CHIPS, get_edge, 0)
        lane = lax.broadcasted_iota(jnp.int32, (512, 128), 1)
        left = jnp.where(chip == 0, 1, 0)
        ours = jnp.where(lax.rem(lane, 16) < 10, left, 1 - left) == 1
        got = edge[...].astype(F32).reshape(512, 128)
        fold = got.reshape(64, 8, 128)
        deep = [pltpu.roll(fold, 2 * s + 2, 1).reshape(512, 128) for s in range(3)]
        deep = [pltpu.roll(deep[s], 64 - 32 * s, 1) for s in range(3)]
        level = row.reshape(512, 128)
        deep = jnp.where(level < 2, deep[0], jnp.where(level < 4, deep[1], deep[2]))
        third, fourth = sent[:, 256:384].astype(F32), sent[:, 384:512].astype(F32)
        sent[:, 256:384] = jnp.where(ours & (lane >= 64), got, third).astype(BF16)
        sent[:, 384:512] = jnp.where(ours, jnp.where(lane < 64, got, deep), fourth).astype(BF16)

    feat[...] = lax.dot_general(
        order_ref[...], sent[...], (((1,), (1,)), ((), ())), preferred_element_type=F32
    ).astype(BF16)

    def back_copy(k):
        return pltpu.make_async_remote_copy(
            src_ref=res.at[k], dst_ref=back.at[chip], send_sem=back_send.at[k], recv_sem=back_recv.at[chip],
            device_id={"scene": 2 * k + c}, device_id_type=MESH,
        )

    def step_of(i):
        zp = lax.rem(z // 2 + far_first(lax.rem(i, 4)), 4)
        return across(x, i // 4) * 4 + zp

    def gather(ref, i):
        ref[...] = jnp.dot(feat[...], hot[step_of(i)], preferred_element_type=F32)

    def sums(ref, i):
        main, halo = [0.0] * 4, [0.0] * 4
        for az in range(AZ):
            a0, b0 = ref[96 * az : 96 * az + 48, 0:256], ref[96 * az : 96 * az + 48, 256:512]
            a1, b1 = ref[96 * az + 48 : 96 * az + 96, 0:256], ref[96 * az + 48 : 96 * az + 96, 256:512]
            planes = (a0 * b0 + a1 * b1, a1 * b0 - a0 * b1, a0 * a0 + a1 * a1, b0 * b0 + b1 * b1)
            for n, plane in enumerate(planes):
                for w in range(4):
                    main[n] = main[n] + plane[8 * w : 8 * w + 8]
                for w in range(4, 6):
                    halo[n] = halo[n] + plane[8 * w : 8 * w + 8]
        looks = [windows(u, v + pltpu.roll(v, 4, 0)) for u, v in zip(main, halo)]
        scale = lax.rsqrt(looks[2] * looks[3] + 1e-06)
        value = jnp.concatenate([looks[0] * scale, looks[1] * scale], axis=0)
        k = 2 * step_of(i)
        res[k] = value[:, 0:128]
        res[k + 1] = value[:, 128:256]

    gather(both_a, 0)

    def compute(j, carry):
        i = 2 * j
        gather(both_b, i + 1)
        sums(both_a, i)
        gather(both_a, lax.rem(i + 2, CHIPS // 2))
        sums(both_b, i + 1)
        for n in range(4):
            k = 2 * step_of(i + n // 2) + n % 2

            @pl.when(k != chip)
            def _():
                back_copy(k).start()
        return carry

    lax.fori_loop(0, CHIPS // 4, compute, 0)
    back[chip] = res[chip]

    def get_back(k, carry):
        @pl.when(k != chip)
        def _():
            pltpu.make_async_remote_copy(
                src_ref=res.at[k], dst_ref=back.at[k], send_sem=back_send.at[k], recv_sem=back_recv.at[k],
                device_id={"scene": 2 * k + c}, device_id_type=MESH,
            ).wait()
        return carry

    gives = []
    for n in range(2):
        h = (x // 2 + 1 + n) % 2
        lax.fori_loop(16 * h, 16 * h + 16, get_back, 0)
        for ri in range(2):
            turned[h, ri] = back[pl.ds(16 * h, 16), 8 * ri : 8 * ri + 8, :].reshape(128, 128).T
        give = pltpu.make_async_remote_copy(
            src_ref=turned.at[h, :, pl.ds(pl.multiple_of(64 * other, 64), 64), :], dst_ref=fin.at[h],
            send_sem=fin_send.at[n], recv_sem=fin_recv.at[n], device_id=partner, device_id_type=MESH,
        )
        give.start()
        gives.append(give)
    for h in range(2):
        out_ref[c, :, :, 128 * h : 128 * h + 128] = turned[h, :, pl.ds(pl.multiple_of(64 * c, 64), 64), :]
    for give in gives:
        give.wait()
    for h in range(2):
        out_ref[other, :, :, 128 * h : 128 * h + 128] = fin[h]


def shards(scene_tiles, scene_slot, pair_ref, pair_sec, pair_count):
    pcap = pair_ref.shape[0]
    order = jnp.asarray(feature_order(), BF16)
    vmem = pl.BlockSpec(memory_space=pltpu.VMEM)
    dma = pltpu.SemaphoreType.DMA
    out = pl.pallas_call(
        kernel,
        out_shape=jax.ShapeDtypeStruct((2, 2, pcap, 256), F32),
        in_specs=[pl.BlockSpec(memory_space=pltpu.HBM)] * 6,
        out_specs=vmem,
        scratch_shapes=[
            pltpu.VMEM((320,), jnp.int32),
            pltpu.VMEM((1, 64), jnp.int32),
            pltpu.VMEM((1, 64), jnp.int32),
            pltpu.VMEM((1, 1), jnp.int32),
            pltpu.VMEM((ROWS, 512), BF16),
            pltpu.VMEM(scene_tiles.shape, BF16),
            pltpu.VMEM((AZ, 16, 1024), BF16),
            pltpu.VMEM((2, AZ, 16, 1280), BF16),
            pltpu.VMEM((CHIPS, 16, 128), BF16),
            pltpu.VMEM((2, 16, 128), BF16),
            pltpu.VMEM((512, 512), BF16),
            pltpu.VMEM((CHIPS, 16, 384), BF16),
            pltpu.VMEM((CHIPS, 16, 384), BF16),
            pltpu.VMEM((2, 128), jnp.int32),
            pltpu.VMEM((2, 128), jnp.int32),
            pltpu.VMEM((2, 128), jnp.int32),
            pltpu.VMEM((CHIPS, 2, 128), jnp.int32),
            pltpu.VMEM((512, 128), jnp.int32),
            pltpu.VMEM((CHIPS // 2, 512, 512), BF16),
            pltpu.VMEM((ROWS, 512), BF16),
            pltpu.VMEM((ROWS, 512), F32),
            pltpu.VMEM((ROWS, 512), F32),
            pltpu.VMEM((CHIPS, 16, 128), F32),
            pltpu.VMEM((CHIPS, 16, 128), F32),
            pltpu.VMEM((2, 2, 128, 128), F32),
            pltpu.VMEM((2, 2, 64, 128), F32),
            dma((6,)), dma((2,)), dma((2,)), dma((2,)), dma((CHIPS,)), dma((CHIPS,)), dma((CHIPS,)),
            dma((CHIPS,)), dma((CHIPS,)), dma((CHIPS,)), dma((CHIPS,)), dma((2,)), dma((2,)),
        ],
        compiler_params=pltpu.CompilerParams(
            collective_id=0, has_side_effects=True, vmem_limit_bytes=54 << 20
        ),
        name="coherence",
    )(scene_tiles, scene_slot, pair_ref.reshape(1, pcap), pair_sec.reshape(1, pcap), pair_count.reshape(1, 1), order)
    return out.transpose(2, 0, 1, 3)


def solution(mesh):
    placed = (P("scene", None, None, "strip"), P(), P("scene"), P("scene"), P("scene"))
    return jax.shard_map(
        shards,
        mesh=mesh,
        in_specs=placed,
        out_specs=P("scene", None, None, "strip"),
        check_vma=False,
    )
```

time: 47.2 us -> 41.9 us (0.89)
  Pallas kernels: 42.8 us -> 39.2 us
  local copies, waits for them, and re-layouts: 3.48 us -> 1.86 us
    pallas_call x1, Pallas kernels: 42.8 us -> 39.2 us  [shards(): pl.pallas_call(kernel, out_shape=jax.ShapeDtypeStruct((2, 2, pcap, 256),...]
    pad x2 -> x0, local copies, waits for them, and re-layouts: 1.23 us -> none  [the longest x1 1.23 us: shards(): tiles = jnp.pad(scene_tiles, ((0, 2), (0, 0), (0, 0), (0, 0)))]
    unnamed x8 -> x0, local copies, waits for them, and re-layouts: 1.23 us -> none
    transpose x1, local copies, waits for them, and re-layouts: 0.91 us -> 1.86 us  [shards(): return out.transpose(2, 0, 1, 3)]
where the time goes in v2:
time: 41.9 us; the launch traced here: 41.7 us
  Pallas kernels  39.2 us (94%)
  local copies, waits for them, and re-layouts  1.86 us (4%)
  between operations  0.66 us (2%)
    pallas_call x1, Pallas kernels, shards(): pl.pallas_call(kernel, out_shape=jax.ShapeDtypeStruct((2, 2, pcap, 256),...  39.2 us
    transpose x1, local copies, waits for them, and re-layouts, shards(): return out.transpose(2, 0, 1, 3)  1.86 us

profile of v2, /device:TPU:1, one launch (start us, length us, event | category | flops | bytes accessed | tf_op | source)
XLA Modules:
  0.0 41.7 jit_solution(5533667962562258216)
XLA Ops:
  0.7 39.2 %coherence.1 = f32[2,2,64,256]{3,2,1,0:T(8,128)} custom-call(bf16[6,10,2,1024]{3,2,1,0:T(2,128)(2,1)} %tiles_hbm.1, s32[320]{0:T(512)} %slot_hbm.1, s32[1,64]{1,0:T(1,128)} %bitcast.6, s32[1,64]{1,0:T(1,128)} %bitcast.7, s32[1,1]{1,0:T(1,128)} %bitcast.4.count_hbm, bf16[480,512]{1,0:T(8,128)(2,1)} %constant.2.clone.order_hbm), custom_call_target="tpu_custom_call" | custom-call | tf_op jit(solution)/shard_map/coherence/pallas_call | solution.py:438
  39.9 1.9 %copy.7 = f32[64,2,2,256]{3,2,1,0:T(2,128)} copy(f32[64,2,2,256]{3,0,2,1:T(8,128)} %bitcast.5) | data formatting | bytes 524288 | tf_op jit(solution)/shard_map/transpose | solution.py:478

commit v3 on v2

--- a/solution.py
+++ b/solution.py
@@ -51,6 +51,11 @@
     return jnp.where(i < 2, 1 - high, high) * 2 + flip
 
 
+def along(z, j):
+    step = (j + 1) // 2
+    return lax.rem(z + jnp.where(lax.rem(j, 2) == 0, ZS // 2 + step, ZS // 2 - step), ZS)
+
+
 def both_parts(v):
     rows = jnp.zeros((2, v.shape[-1]), F32)
     v = v.astype(F32)
@@ -68,9 +73,10 @@
 
 def kernel(
     tiles_hbm, slot_hbm, ref_hbm, sec_hbm, count_hbm, order_hbm, out_ref,
-    slot_ref, ref_ref, sec_ref, count_ref, order_ref, raw, pre, ext, edge, edge_msg, sent, msg, land, own_list, lst, chip_list, lists, scene_k, hot, feat, both_a, both_b,
+    slot_ref, ref_ref, sec_ref, count_ref, order_ref, raw, ext, edge, edge_par, edge_msg, sent, msg, land, par,
+    own_list, lists, lists_par, scene_k, hot, feat, both_a, both_b,
     res, back, turned, fin,
-    in_sem, core_send, core_recv, edge_send, edge_recv, list_send, list_recv,
+    in_sem, core_send, core_recv, hand_send, hand_recv, edge_send, edge_recv, list_send, list_recv,
     data_send, data_recv, back_send, back_recv, fin_send, fin_recv,
 ):
     me = lax.axis_index("scene")
@@ -126,61 +132,21 @@
     gets[0].wait()
 
     def lines(az, carry):
-        pre[az] = both_parts(raw[:, 5 * other + az])
-        ext[c, az, :, 128:1152] = both_parts(raw[:, 5 * c + az])
+        for line in range(2):
+            ext[line, az, :, 128:1152] = both_parts(raw[:, AZ * line + az])
         return carry
 
     lax.fori_loop(0, AZ, lines, 0)
-    sides = jnp.where(y < STRIPS - 1, 1, 0) + jnp.where(y > 0, 1, 0)
-    pl.semaphore_wait(barrier, CHIPS + sides)
-
-    give_line = pltpu.make_async_remote_copy(
-        src_ref=pre, dst_ref=ext.at[c, :, :, pl.ds(128, 1024)],
-        send_sem=core_send.at[1], recv_sem=core_recv.at[1], device_id=partner, device_id_type=MESH,
-    )
-    give_line.start()
-    give_list = pltpu.make_async_remote_copy(
-        src_ref=own_list, dst_ref=lst, send_sem=core_send.at[0], recv_sem=core_recv.at[0],
-        device_id=partner, device_id_type=MESH,
-    )
-    give_list.start()
-
-    give_list.wait()
-    half = lax.broadcasted_iota(jnp.int32, (2, 128), 1) // 64
-    chip_list[...] = jnp.where(half == c, own_list[...], lst[...])
-    lists[chip] = chip_list[...]
-
-    def list_copy(k):
-        return pltpu.make_async_remote_copy(
-            src_ref=chip_list, dst_ref=lists.at[chip], send_sem=list_send.at[k], recv_sem=list_recv.at[chip],
-            device_id={"scene": 2 * k + c}, device_id_type=MESH,
-        )
-
-    def send_list(i, carry):
-        k = across(x, i // ZS) * ZS + lax.rem(z + 4 + i, ZS)
-
-        @pl.when(k != chip)
-        def _():
-            list_copy(k).start()
-        return carry
-
-    give_line.wait()
 
     lanes = lax.broadcasted_iota(jnp.int32, (16, 128), 1)
     in32 = lax.rem(lanes, 32)
     row8 = lax.broadcasted_iota(jnp.int32, (2, 8, 128), 1)
 
-    def data_copy(k):
-        return pltpu.make_async_remote_copy(
-            src_ref=msg.at[k], dst_ref=land.at[chip], send_sem=data_send.at[k], recv_sem=data_recv.at[chip],
-            device_id={"scene": 2 * k + c}, device_id_type=MESH,
-        )
-
-    def pack(t):
+    def pack(t, carry):
         at = pl.ds(pl.multiple_of(t * 128, 128), 384)
         groups, halos = [], []
         for az in range(AZ):
-            v = [ext[core, az, :, at].astype(F32) for core in range(2)]
+            v = [ext[line, az, :, at].astype(F32) for line in range(2)]
             re = jnp.concatenate([v[0][0:8], v[1][0:8]], axis=0)
             im = jnp.concatenate([v[0][8:16], v[1][8:16]], axis=0)
             groups += [re[:, 128:256], im[:, 128:256]]
@@ -209,25 +175,15 @@
                 tile = turned4[s][sub].reshape(2, 8, 128)
                 tile = jnp.where(row8 >= 6, pltpu.roll(last, 6 - 2 * s, 1), tile)
                 msg[k, :, 128 * s : 128 * s + 128] = tile.reshape(16, 128).astype(BF16)
-        for sub in range(4):
-            k = 4 * t + sub
-
-            @pl.when(k != chip)
-            def _():
-                data_copy(k).start()
-
-    def tile_at(i):
-        first = 1 - z // 4
-        return across(x, i // 2) * 2 + jnp.where(lax.rem(i, 2) == 0, first, 1 - first)
-
-    def pack_at(i, carry):
-        pack(tile_at(i))
-        return carry
+        return carry
+
+    lax.fori_loop(0, TILES, pack, 0)
+    land[chip] = msg[chip]
 
     def edge_pack(n, start):
         whole = jnp.zeros((16, 128), F32)
         for az in range(AZ):
-            v = [ext[core, az, :, start : start + 128].astype(F32) for core in range(2)]
+            v = [ext[line, az, :, start : start + 128].astype(F32) for line in range(2)]
             re = jnp.concatenate([v[0][0:8], v[1][0:8]], axis=0)
             im = jnp.concatenate([v[0][8:16], v[1][8:16]], axis=0)
             for s in range(3 if az == 4 else 1):
@@ -243,13 +199,14 @@
 
     def edge_copy(n, to, row):
         return pltpu.make_async_remote_copy(
-            src_ref=edge_msg.at[n], dst_ref=edge.at[chip], send_sem=edge_send.at[n], recv_sem=edge_recv.at[chip],
+            src_ref=edge_msg.at[n], dst_ref=edge.at[chip], send_sem=edge_send.at[n], recv_sem=edge_recv,
             device_id={"scene": 2 * to + c, "strip": row}, device_id_type=MESH,
         )
 
-    pack_at(0, 0)
     edge_pack(0, 1024)
     edge_pack(1, 128)
+    sides = jnp.where(y < STRIPS - 1, 1, 0) + jnp.where(y > 0, 1, 0)
+    pl.semaphore_wait(barrier, CHIPS + sides)
 
     @pl.when(y < STRIPS - 1)
     def _():
@@ -259,19 +216,26 @@
     def _():
         edge_copy(1, CHIPS - 1, y - 1).start()
 
-    lax.fori_loop(1, 3, pack_at, 0)
-    lax.fori_loop(0, CHIPS, send_list, 0)
-    lax.fori_loop(3, TILES, pack_at, 0)
-
-    @pl.when(y < STRIPS - 1)
-    def _():
-        edge_copy(0, 0, y + 1).wait_send()
-
-    @pl.when(y > 0)
-    def _():
-        edge_copy(1, CHIPS - 1, y - 1).wait_send()
-
-    land[chip] = msg[chip]
+    order = [across(x, i // ZS) * ZS + along(z, i % ZS) for i in range(CHIPS - 1)]
+
+    def data_copy(i, src, dst, to):
+        return pltpu.make_async_remote_copy(
+            src_ref=src, dst_ref=dst, send_sem=data_send, recv_sem=data_recv.at[i],
+            device_id={"scene": 2 * to + c}, device_id_type=MESH,
+        )
+
+    def list_copy(src, dst, to):
+        return pltpu.make_async_remote_copy(
+            src_ref=src, dst_ref=dst, send_sem=list_send, recv_sem=list_recv,
+            device_id={"scene": 2 * to + c}, device_id_type=MESH,
+        )
+
+    for i in range(ZS):
+        data_copy(i // ZS, msg.at[order[i]], land.at[chip], order[i]).start()
+    for i in range(CHIPS - 1):
+        list_copy(own_list, lists.at[chip], order[i]).start()
+    for i in range(ZS, CHIPS - 1):
+        data_copy(i // ZS, msg.at[order[i]], land.at[chip], order[i]).start()
 
     gets[4].wait()
     gets[5].wait()
@@ -284,61 +248,82 @@
     scene = jnp.sum(jnp.where(slot == slot_ref[...].reshape(1, 320), lane + 1.0, 0.0), axis=1, keepdims=True) - 1.0
     scene_k[...] = jnp.broadcast_to(scene, (512, 128)).astype(jnp.int32)
 
-    def get_list(k, carry):
-        @pl.when(k != chip)
-        def _():
-            pltpu.make_async_remote_copy(
-                src_ref=chip_list, dst_ref=lists.at[k], send_sem=list_send.at[k], recv_sem=list_recv.at[k],
-                device_id={"scene": 2 * k + c}, device_id_type=MESH,
-            ).wait()
-        return carry
-
-    lax.fori_loop(0, CHIPS, get_list, 0)
+    lists[chip] = own_list[...]
+
+    def hand(i):
+        first = across(x, i) * ZS
+        many = ZS if i < XS - 1 else ZS - 1
+        data_copy(i, msg.at[pl.ds(0, many)], land.at[pl.ds(first, many)], chip).wait_recv()
+        copy = pltpu.make_async_remote_copy(
+            src_ref=land.at[pl.ds(first, ZS)], dst_ref=par.at[pl.ds(first, ZS)],
+            send_sem=hand_send.at[i], recv_sem=hand_recv.at[i], device_id=partner, device_id_type=MESH,
+        )
+        copy.start()
+        return copy
+
+    most = pl.ds(0, CHIPS - 1)
+    list_copy(lists.at[most], lists.at[most], chip).wait_recv()
+    hand_list = pltpu.make_async_remote_copy(
+        src_ref=lists, dst_ref=lists_par, send_sem=core_send.at[0], recv_sem=core_recv.at[0],
+        device_id=partner, device_id_type=MESH,
+    )
+    hand_list.start()
+    hands = [hand(0)]
+    hand_list.wait()
+
+    half = lax.broadcasted_iota(jnp.int32, (2, 128), 1) // 64
 
     def one_hot(m, carry):
         for n in range(2):
-            pair = lists[2 * m + n]
+            pair = jnp.where(half == c, lists[2 * m + n], lists_par[2 * m + n])
             for part in range(2):
                 hit = jnp.where(scene_k[...] == pair[part : part + 1, :], 1.0, 0.0).astype(BF16)
                 hot[m, :, 256 * part + 128 * n : 256 * part + 128 * n + 128] = hit
         return carry
 
     lax.fori_loop(0, CHIPS // 2, one_hot, 0)
-
-    def get_data(k, carry):
-        @pl.when(k != chip)
-        def _():
-            pltpu.make_async_remote_copy(
-                src_ref=msg.at[k], dst_ref=land.at[k], send_sem=data_send.at[k], recv_sem=data_recv.at[k],
-                device_id={"scene": 2 * k + c}, device_id_type=MESH,
-            ).wait()
-        return carry
-
-    lax.fori_loop(0, CHIPS, get_data, 0)
-
-    part = [land[:, :, 128 * s : 128 * s + 128].reshape(512, 128) for s in range(3)]
-    wide = [p.astype(F32).reshape(64, 8, 128) for p in part]
+    hands.append(hand(1))
+    hand_edge = pltpu.make_async_remote_copy(
+        src_ref=edge, dst_ref=edge_par, send_sem=core_send.at[1], recv_sem=core_recv.at[1],
+        device_id=partner, device_id_type=MESH,
+    )
+
+    @pl.when(at_left | at_right)
+    def _():
+        pltpu.make_async_remote_copy(
+            src_ref=edge, dst_ref=edge, send_sem=edge_send.at[0], recv_sem=edge_recv,
+            device_id={"scene": 2 * chip + c, "strip": side}, device_id_type=MESH,
+        ).wait_recv()
+        hand_edge.start()
+
+    hands.append(hand(2))
+    hands.append(hand(3))
+    for copy in hands:
+        copy.wait()
+
+    def line_of(mine, others):
+        a, b = (v.astype(F32).reshape(CHIPS, 2, 8, 128) for v in (mine, others))
+        a = jnp.where(c == 0, a[:, 0], a[:, 1])
+        b = jnp.where(c == 0, b[:, 0], b[:, 1])
+        pair = [jnp.where(c == 0, a, b), jnp.where(c == 0, b, a)]
+        return jnp.stack(pair, axis=1).reshape(64, 8, 128)
+
+    wide = [line_of(*(r[:, :, 128 * s : 128 * s + 128] for r in (land, par))) for s in range(3)]
+    part = [v.reshape(512, 128).astype(BF16) for v in wide]
     row = lax.broadcasted_iota(jnp.int32, (64, 8, 128), 1)
     last = jnp.where(
         row < 2, pltpu.roll(wide[0], 2, 1), jnp.where(row < 4, pltpu.roll(wide[1], 4, 1), pltpu.roll(wide[2], 6, 1))
     )
     sent[...] = jnp.concatenate(part + [last.reshape(512, 128).astype(BF16)], axis=1)
 
-    def get_edge(k, carry):
-        pltpu.make_async_remote_copy(
-            src_ref=edge_msg.at[0], dst_ref=edge.at[k], send_sem=edge_send.at[0], recv_sem=edge_recv.at[k],
-            device_id={"scene": 2 * k + c, "strip": side}, device_id_type=MESH,
-        ).wait_recv()
-        return carry
-
     @pl.when(at_left | at_right)
     def _():
-        lax.fori_loop(0, CHIPS, get_edge, 0)
+        hand_edge.wait()
         lane = lax.broadcasted_iota(jnp.int32, (512, 128), 1)
         left = jnp.where(chip == 0, 1, 0)
         ours = jnp.where(lax.rem(lane, 16) < 10, left, 1 - left) == 1
-        got = edge[...].astype(F32).reshape(512, 128)
-        fold = got.reshape(64, 8, 128)
+        fold = line_of(edge[...], edge_par[...])
+        got = fold.reshape(512, 128)
         deep = [pltpu.roll(fold, 2 * s + 2, 1).reshape(512, 128) for s in range(3)]
         deep = [pltpu.roll(deep[s], 64 - 32 * s, 1) for s in range(3)]
         level = row.reshape(512, 128)
@@ -351,10 +336,10 @@
         order_ref[...], sent[...], (((1,), (1,)), ((), ())), preferred_element_type=F32
     ).astype(BF16)
 
-    def back_copy(k):
+    def back_copy(i, src, dst, to):
         return pltpu.make_async_remote_copy(
-            src_ref=res.at[k], dst_ref=back.at[chip], send_sem=back_send.at[k], recv_sem=back_recv.at[chip],
-            device_id={"scene": 2 * k + c}, device_id_type=MESH,
+            src_ref=src, dst_ref=dst, send_sem=back_send, recv_sem=back_recv.at[i],
+            device_id={"scene": 2 * to + c}, device_id_type=MESH,
         )
 
     def step_of(i):
@@ -395,25 +380,18 @@
 
             @pl.when(k != chip)
             def _():
-                back_copy(k).start()
+                back_copy(j // 2, res.at[k], back.at[chip], k).start()
         return carry
 
     lax.fori_loop(0, CHIPS // 4, compute, 0)
     back[chip] = res[chip]
-
-    def get_back(k, carry):
-        @pl.when(k != chip)
-        def _():
-            pltpu.make_async_remote_copy(
-                src_ref=res.at[k], dst_ref=back.at[k], send_sem=back_send.at[k], recv_sem=back_recv.at[k],
-                device_id={"scene": 2 * k + c}, device_id_type=MESH,
-            ).wait()
-        return carry
 
     gives = []
     for n in range(2):
         h = (x // 2 + 1 + n) % 2
-        lax.fori_loop(16 * h, 16 * h + 16, get_back, 0)
+        for i in (2 * n, 2 * n + 1):
+            some = pl.ds(0, ZS if i < XS - 1 else ZS - 1)
+            back_copy(i, res.at[some], back.at[some], chip).wait_recv()
         for ri in range(2):
             turned[h, ri] = back[pl.ds(16 * h, 16), 8 * ri : 8 * ri + 8, :].reshape(128, 128).T
         give = pltpu.make_async_remote_copy(
@@ -428,6 +406,18 @@
         give.wait()
     for h in range(2):
         out_ref[other, :, :, 128 * h : 128 * h + 128] = fin[h]
+
+    @pl.when(y < STRIPS - 1)
+    def _():
+        edge_copy(0, 0, y + 1).wait_send()
+
+    @pl.when(y > 0)
+    def _():
+        edge_copy(1, CHIPS - 1, y - 1).wait_send()
+
+    list_copy(lists.at[most], lists.at[most], chip).wait_send()
+    data_copy(0, msg.at[most], land.at[most], chip).wait_send()
+    back_copy(0, res.at[most], back.at[most], chip).wait_send()
 
 
 def shards(scene_tiles, scene_slot, pair_ref, pair_sec, pair_count):
@@ -447,16 +437,16 @@
             pltpu.VMEM((1, 1), jnp.int32),
             pltpu.VMEM((ROWS, 512), BF16),
             pltpu.VMEM(scene_tiles.shape, BF16),
-            pltpu.VMEM((AZ, 16, 1024), BF16),
             pltpu.VMEM((2, AZ, 16, 1280), BF16),
+            pltpu.VMEM((CHIPS, 16, 128), BF16),
             pltpu.VMEM((CHIPS, 16, 128), BF16),
             pltpu.VMEM((2, 16, 128), BF16),
             pltpu.VMEM((512, 512), BF16),
             pltpu.VMEM((CHIPS, 16, 384), BF16),
             pltpu.VMEM((CHIPS, 16, 384), BF16),
+            pltpu.VMEM((CHIPS, 16, 384), BF16),
             pltpu.VMEM((2, 128), jnp.int32),
-            pltpu.VMEM((2, 128), jnp.int32),
-            pltpu.VMEM((2, 128), jnp.int32),
+            pltpu.VMEM((CHIPS, 2, 128), jnp.int32),
             pltpu.VMEM((CHIPS, 2, 128), jnp.int32),
             pltpu.VMEM((512, 128), jnp.int32),
             pltpu.VMEM((CHIPS // 2, 512, 512), BF16),
@@ -467,8 +457,8 @@
             pltpu.VMEM((CHIPS, 16, 128), F32),
             pltpu.VMEM((2, 2, 128, 128), F32),
             pltpu.VMEM((2, 2, 64, 128), F32),
-            dma((6,)), dma((2,)), dma((2,)), dma((2,)), dma((CHIPS,)), dma((CHIPS,)), dma((CHIPS,)),
-            dma((CHIPS,)), dma((CHIPS,)), dma((CHIPS,)), dma((CHIPS,)), dma((2,)), dma((2,)),
+            dma((6,)), dma((2,)), dma((2,)), dma((XS,)), dma((XS,)), dma((2,)), dma, dma, dma,
+            dma, dma((XS,)), dma, dma((XS,)), dma((2,)), dma((2,)),
         ],
         compiler_params=pltpu.CompilerParams(
             collective_id=0, has_side_effects=True, vmem_limit_bytes=54 << 20

time: 41.9 us -> 39.3 us (0.938)
  Pallas kernels: 39.2 us -> 36.6 us
    pallas_call x1, Pallas kernels: 39.2 us -> 36.6 us  [shards(): pl.pallas_call(kernel, out_shape=jax.ShapeDtypeStruct((2, 2, pcap, 256),...]
where the time goes in v3:
time: 39.3 us; the launch traced here: 39.1 us
  Pallas kernels  36.6 us (93%)
  local copies, waits for them, and re-layouts  1.86 us (5%)
  between operations  0.66 us (2%)
    pallas_call x1, Pallas kernels, shards(): pl.pallas_call(kernel, out_shape=jax.ShapeDtypeStruct((2, 2, pcap, 256),...  36.6 us
    transpose x1, local copies, waits for them, and re-layouts, shards(): return out.transpose(2, 0, 1, 3)  1.86 us

profile of v3, /device:TPU:1, one launch (start us, length us, event | category | flops | bytes accessed | tf_op | source)
XLA Modules:
  0.0 39.1 jit_solution(11113428538132022067)
XLA Ops:
  0.7 36.6 %coherence.1 = f32[2,2,64,256]{3,2,1,0:T(8,128)} custom-call(bf16[6,10,2,1024]{3,2,1,0:T(2,128)(2,1)} %tiles_hbm.1, s32[320]{0:T(512)} %slot_hbm.1, s32[1,64]{1,0:T(1,128)} %bitcast.6, s32[1,64]{1,0:T(1,128)} %bitcast.7, s32[1,1]{1,0:T(1,128)} %bitcast.4.count_hbm, bf16[480,512]{1,0:T(8,128)(2,1)} %constant.2.clone.order_hbm), custom_call_target="tpu_custom_call" | custom-call | tf_op jit(solution)/shard_map/coherence/pallas_call | solution.py:428
  37.3 1.9 %copy.7 = f32[64,2,2,256]{3,2,1,0:T(2,128)} copy(f32[64,2,2,256]{3,0,2,1:T(8,128)} %bitcast.5) | data formatting | bytes 524288 | tf_op jit(solution)/shard_map/transpose | solution.py:468

commit v4 on v3

--- a/solution.py
+++ b/solution.py
@@ -367,13 +367,11 @@
         res[k] = value[:, 0:128]
         res[k + 1] = value[:, 128:256]
 
-    gather(both_a, 0)
-
     def compute(j, carry):
         i = 2 * j
+        gather(both_a, i)
+        sums(both_a, i)
         gather(both_b, i + 1)
-        sums(both_a, i)
-        gather(both_a, lax.rem(i + 2, CHIPS // 2))
         sums(both_b, i + 1)
         for n in range(4):
             k = 2 * step_of(i + n // 2) + n % 2
@@ -425,6 +423,10 @@
     order = jnp.asarray(feature_order(), BF16)
     vmem = pl.BlockSpec(memory_space=pltpu.VMEM)
     dma = pltpu.SemaphoreType.DMA
+    arrays = (
+        scene_tiles, scene_slot, pair_ref.reshape(1, pcap), pair_sec.reshape(1, pcap),
+        pair_count.reshape(1, 1), order,
+    )
     out = pl.pallas_call(
         kernel,
         out_shape=jax.ShapeDtypeStruct((2, 2, pcap, 256), F32),
@@ -461,10 +463,10 @@
             dma, dma((XS,)), dma, dma((XS,)), dma((2,)), dma((2,)),
         ],
         compiler_params=pltpu.CompilerParams(
-            collective_id=0, has_side_effects=True, vmem_limit_bytes=54 << 20
+            collective_id=0, has_side_effects=True, vmem_limit_bytes=40 << 20
         ),
         name="coherence",
-    )(scene_tiles, scene_slot, pair_ref.reshape(1, pcap), pair_sec.reshape(1, pcap), pair_count.reshape(1, 1), order)
+    )(*(v if v.size == 1 else pltpu.with_memory_space_constraint(v, pltpu.HBM) for v in arrays))
     return out.transpose(2, 0, 1, 3)
 
 

time: 39.3 us -> 37.7 us (0.959)
  local copies, waits for them, and re-layouts: 1.86 us -> 0.91 us
  Pallas kernels: 36.6 us -> 36 us
    transpose x1, local copies, waits for them, and re-layouts: 1.86 us -> 0.91 us  [shards(): return out.transpose(2, 0, 1, 3)]
    pallas_call x1, Pallas kernels: 36.6 us -> 36 us  [shards(): pl.pallas_call(kernel, out_shape=jax.ShapeDtypeStruct((2, 2, pcap, 256),...]
where the time goes in v4:
time: 37.7 us; the launch traced here: 37.6 us
  Pallas kernels  36 us (95%)
  local copies, waits for them, and re-layouts  0.91 us (2%)
  between operations  0.66 us (2%)
    pallas_call x1, Pallas kernels, shards(): pl.pallas_call(kernel, out_shape=jax.ShapeDtypeStruct((2, 2, pcap, 256),...  36 us
    transpose x1, local copies, waits for them, and re-layouts, shards(): return out.transpose(2, 0, 1, 3)  0.91 us

profile of v4, /device:TPU:1, one launch (start us, length us, event | category | flops | bytes accessed | tf_op | source)
XLA Modules:
  0.0 37.6 jit_solution(9158423652903555756)
XLA Ops:
  0.7 36.0 %coherence.1 = f32[2,2,64,256]{3,2,1,0:T(8,128)S(1)} custom-call(bf16[6,10,2,1024]{3,2,1,0:T(2,128)(2,1)} %tiles_hbm.1, s32[320]{0:T(512)} %slot_hbm.1, s32[1,64]{1,0:T(1,128)} %bitcast.6, s32[1,64]{1,0:T(1,128)} %bitcast.7, s32[1,1]{1,0:T(1,128)} %bitcast.4.count_hbm, bf16[480,512]{1,0:T(8,128)(2,1)} %constant.2.clone.order_hbm), custom_call_target="tpu_custom_call" | custom-call | tf_op jit(solution)/shard_map/coherence/pallas_call | solution.py:430
  36.7 0.9 %copy.7 = f32[64,2,2,256]{3,2,1,0:T(2,128)} copy(f32[64,2,2,256]{3,0,2,1:T(8,128)S(1)} %bitcast.5) | data formatting | bytes 524288 | tf_op jit(solution)/shard_map/transpose | solution.py:470

commit v5 on v4

--- a/solution.py
+++ b/solution.py
@@ -269,7 +269,7 @@
     )
     hand_list.start()
     hands = [hand(0)]
-    hand_list.wait()
+    hand_list.wait_recv()
 
     half = lax.broadcasted_iota(jnp.int32, (2, 128), 1) // 64
 
@@ -299,7 +299,7 @@
     hands.append(hand(2))
     hands.append(hand(3))
     for copy in hands:
-        copy.wait()
+        copy.wait_recv()
 
     def line_of(mine, others):
         a, b = (v.astype(F32).reshape(CHIPS, 2, 8, 128) for v in (mine, others))
@@ -350,22 +350,23 @@
         ref[...] = jnp.dot(feat[...], hot[step_of(i)], preferred_element_type=F32)
 
     def sums(ref, i):
-        main, halo = [0.0] * 4, [0.0] * 4
-        for az in range(AZ):
-            a0, b0 = ref[96 * az : 96 * az + 48, 0:256], ref[96 * az : 96 * az + 48, 256:512]
-            a1, b1 = ref[96 * az + 48 : 96 * az + 96, 0:256], ref[96 * az + 48 : 96 * az + 96, 256:512]
-            planes = (a0 * b0 + a1 * b1, a1 * b0 - a0 * b1, a0 * a0 + a1 * a1, b0 * b0 + b1 * b1)
-            for n, plane in enumerate(planes):
-                for w in range(4):
-                    main[n] = main[n] + plane[8 * w : 8 * w + 8]
-                for w in range(4, 6):
-                    halo[n] = halo[n] + plane[8 * w : 8 * w + 8]
-        looks = [windows(u, v + pltpu.roll(v, 4, 0)) for u, v in zip(main, halo)]
-        scale = lax.rsqrt(looks[2] * looks[3] + 1e-06)
-        value = jnp.concatenate([looks[0] * scale, looks[1] * scale], axis=0)
-        k = 2 * step_of(i)
-        res[k] = value[:, 0:128]
-        res[k + 1] = value[:, 128:256]
+        for n in range(2):
+            p, q = slice(128 * n, 128 * n + 128), slice(256 + 128 * n, 384 + 128 * n)
+            main, halo = [0.0] * 4, [0.0] * 4
+            for az in range(AZ):
+                a0, b0 = ref[96 * az : 96 * az + 48, p], ref[96 * az : 96 * az + 48, q]
+                a1, b1 = ref[96 * az + 48 : 96 * az + 96, p], ref[96 * az + 48 : 96 * az + 96, q]
+                planes = (a0 * b0 + a1 * b1, a1 * b0 - a0 * b1, a0 * a0 + a1 * a1, b0 * b0 + b1 * b1)
+                for m, plane in enumerate(planes):
+                    for w in range(4):
+                        main[m] = main[m] + plane[8 * w : 8 * w + 8]
+                    for w in range(4, 6):
+                        halo[m] = halo[m] + plane[8 * w : 8 * w + 8]
+            looks = [windows(u, v + pltpu.roll(v, 4, 0)) for u, v in zip(main, halo)]
+            scale = lax.rsqrt(looks[2] * looks[3] + 1e-06)
+            value = jnp.concatenate([looks[0] * scale, looks[1] * scale], axis=0)
+            res[2 * step_of(i) + n] = value
+
 
     def compute(j, carry):
         i = 2 * j
@@ -400,6 +401,8 @@
         gives.append(give)
     for h in range(2):
         out_ref[c, :, :, 128 * h : 128 * h + 128] = turned[h, :, pl.ds(pl.multiple_of(64 * c, 64), 64), :]
+    for copy in hands + [hand_list]:
+        copy.wait_send()
     for give in gives:
         give.wait()
     for h in range(2):

time: 37.7 us -> 37.4 us (level)
  no operation moved by 1% of the time
where the time goes in v5:
time: 37.4 us; the launch traced here: 37.3 us
  Pallas kernels  35.7 us (95%)
  local copies, waits for them, and re-layouts  0.91 us (2%)
  between operations  0.66 us (2%)
    pallas_call x1, Pallas kernels, shards(): pl.pallas_call(kernel, out_shape=jax.ShapeDtypeStruct((2, 2, pcap, 256),...  35.7 us
    transpose x1, local copies, waits for them, and re-layouts, shards(): return out.transpose(2, 0, 1, 3)  0.91 us

profile of v5, /device:TPU:1, one launch (start us, length us, event | category | flops | bytes accessed | tf_op | source)
XLA Modules:
  0.0 37.3 jit_solution(14844818768311001012)
XLA Ops:
  0.7 35.7 %coherence.1 = f32[2,2,64,256]{3,2,1,0:T(8,128)S(1)} custom-call(bf16[6,10,2,1024]{3,2,1,0:T(2,128)(2,1)} %tiles_hbm.1, s32[320]{0:T(512)} %slot_hbm.1, s32[1,64]{1,0:T(1,128)} %bitcast.6, s32[1,64]{1,0:T(1,128)} %bitcast.7, s32[1,1]{1,0:T(1,128)} %bitcast.4.count_hbm, bf16[480,512]{1,0:T(8,128)(2,1)} %constant.2.clone.order_hbm), custom_call_target="tpu_custom_call" | custom-call | tf_op jit(solution)/shard_map/coherence/pallas_call | solution.py:433
  36.4 0.9 %copy.7 = f32[64,2,2,256]{3,2,1,0:T(2,128)} copy(f32[64,2,2,256]{3,0,2,1:T(8,128)S(1)} %bitcast.5) | data formatting | bytes 524288 | tf_op jit(solution)/shard_map/transpose | solution.py:473

commit v6 on v5

--- a/solution.py
+++ b/solution.py
@@ -88,14 +88,10 @@
 
     barrier = pltpu.get_barrier_semaphore()
 
-    def greet(k, carry):
-        @pl.when(k != chip)
-        def _():
-            pl.semaphore_signal(barrier, inc=1, device_id={"scene": 2 * k + c}, device_id_type=MESH)
-        return carry
-
+    order = [across(x, i // ZS) * ZS + along(z, i % ZS) for i in range(CHIPS - 1)]
+    for k in order:
+        pl.semaphore_signal(barrier, inc=1, device_id={"scene": 2 * k + c}, device_id_type=MESH)
     pl.semaphore_signal(barrier, inc=1, device_id=partner, device_id_type=MESH)
-    lax.fori_loop(0, CHIPS, greet, 0)
 
     at_left = (chip == 0) & (y > 0)
     at_right = (chip == CHIPS - 1) & (y < STRIPS - 1)
@@ -215,8 +211,6 @@
     @pl.when(y > 0)
     def _():
         edge_copy(1, CHIPS - 1, y - 1).start()
-
-    order = [across(x, i // ZS) * ZS + along(z, i % ZS) for i in range(CHIPS - 1)]
 
     def data_copy(i, src, dst, to):
         return pltpu.make_async_remote_copy(

time: 37.4 us -> 37.3 us (level)
  no operation moved by 1% of the time
where the time goes in v6:
time: 37.3 us; the launch traced here: 37.2 us
  Pallas kernels  35.7 us (96%)
  local copies, waits for them, and re-layouts  0.91 us (2%)
  between operations  0.66 us (2%)
    pallas_call x1, Pallas kernels, shards(): pl.pallas_call(kernel, out_shape=jax.ShapeDtypeStruct((2, 2, pcap, 256),...  35.7 us
    transpose x1, local copies, waits for them, and re-layouts, shards(): return out.transpose(2, 0, 1, 3)  0.91 us

profile of v6, /device:TPU:1, one launch (start us, length us, event | category | flops | bytes accessed | tf_op | source)
XLA Modules:
  0.0 37.2 jit_solution(9550297680743871485)
XLA Ops:
  0.7 35.7 %coherence.1 = f32[2,2,64,256]{3,2,1,0:T(8,128)S(1)} custom-call(bf16[6,10,2,1024]{3,2,1,0:T(2,128)(2,1)} %tiles_hbm.1, s32[320]{0:T(512)} %slot_hbm.1, s32[1,64]{1,0:T(1,128)} %bitcast.6, s32[1,64]{1,0:T(1,128)} %bitcast.7, s32[1,1]{1,0:T(1,128)} %bitcast.4.count_hbm, bf16[480,512]{1,0:T(8,128)(2,1)} %constant.2.clone.order_hbm), custom_call_target="tpu_custom_call" | custom-call | tf_op jit(solution)/shard_map/coherence/pallas_call | solution.py:427
  36.3 0.9 %copy.7 = f32[64,2,2,256]{3,2,1,0:T(2,128)} copy(f32[64,2,2,256]{3,0,2,1:T(8,128)S(1)} %bitcast.5) | data formatting | bytes 524288 | tf_op jit(solution)/shard_map/transpose | solution.py:467
